TPU v7x, 128 devices: a whole 4x4x4 slice. The times are simulated.
128 devices in a mesh: arc: 8 (over x_hi, z), col: 16 (over x_lo, y, core).
Axes of the slice: x: 4 (x_hi: 2, x_lo: 2; x = x_hi * 2 + x_lo), y: 4, z: 4, core: 2. Of those that a mesh axis runs over, the one named last changes fastest.
Arguments:
- local_obs: float32 [1024, 320, 128], P(('arc', 'col')), may hold values from -6 to 6
- global_obs: float32 [1024, 320, 512], P('arc', None, 'col'), may hold values from -0.75 to 0.75
- row_counts: int32 [1024], P('arc'), may hold values from 160 to 320, as said below
- owner_map: int32 [1024], P(('arc', 'col')), may hold values from 0 to 255, as said below
- prior_factor: float32 [256, 512, 512], P(('arc', 'col')), as said below
Outputs:
- updated_factor: float32 [256, 512, 512], P(('arc', 'col'))
Inputs may be any that keep to these rules, and one draw needn't show every extreme that they name: `row_counts`: between 160 and 320; some arc has exactly 320 rows and another exactly 160. `owner_map`: the slice of arc k lies on a device with the same col index as the device that holds local_obs[k]; slice s lies on device s // 2 in arc+col order; from the 8 arcs of one device at most 2 have slices on devices of one arc index, and exactly 2 on one of them; in each col index one device receives 2 arcs from every device of that col index. `prior_factor`: each slice's factor is upper triangular with a positive diagonal.
All inputs are finite; a program needn't handle non-finite values.
Results may differ from a plain program's by a relative error of at most 0.0003.
Values sent between devices are 32-bit elements; how exact they have to be, the bound alone decides.
No kernel may reach another device: no remote copies, remote signals or barrier semaphores. Data moves between devices by JAX's collectives and lax.ppermute only.
A program may use at most 128 MiB of HBM per device.

v0:
```python
import jax
import jax.numpy as jnp
from jax import lax
from jax.sharding import PartitionSpec as P

SLICE_DEV = 2


highest_precision = lax.Precision.HIGHEST


def valid_row_mask(counts, maximum_row_count):
    places = lax.broadcasted_iota(jnp.int32, (counts.shape[0], maximum_row_count, 1), 1)
    return (places < counts[:, None, None]).astype(jnp.float32)


def orthonormal(local_part, weight_valid_mask):
    masked = local_part * weight_valid_mask
    local_gram = jnp.einsum("arl,arm->alm", masked, masked, precision=highest_precision)
    factor_low = jnp.linalg.cholesky(local_gram)
    return lax.linalg.triangular_solve(
        factor_low, masked, left_side=False, lower=True, transpose_a=True
    )


def eliminate_local_block(basis_vectors, global_block):
    coupling = jnp.einsum("arl,arc->alc", basis_vectors, global_block, precision=highest_precision)
    return global_block - jnp.einsum(
        "arl,alc->arc", basis_vectors, coupling, precision=highest_precision
    )


def per_device(local_obs, global_obs, row_counts, owner_map, prior_factor):
    arc_dev = local_obs.shape[0]
    maximum_row_count = local_obs.shape[1]
    slice_width = prior_factor.shape[1]
    arc_groups = lax.axis_size("arc")
    col_groups = lax.axis_size("col")
    column = lax.axis_index("col")
    owned_row_counts = lax.dynamic_slice_in_dim(row_counts, column * arc_dev, arc_dev)
    basis_vectors = orthonormal(local_obs, valid_row_mask(owned_row_counts, maximum_row_count))
    combined_matrix = lax.all_to_all(global_obs, "col", split_axis=0, concat_axis=2, tiled=True)
    remaining_columns = eliminate_local_block(
        basis_vectors, combined_matrix * valid_row_mask(owned_row_counts, maximum_row_count)
    )
    target_dev = owner_map // SLICE_DEV
    target_arc = target_dev // col_groups
    target_slice = owner_map % SLICE_DEV
    capacity = max(2, arc_dev // 4)
    indices = jnp.arange(arc_dev, dtype=jnp.int32)
    earlier = (target_arc[None, :] == target_arc[:, None]) & (indices[None, :] < indices[:, None])
    slot_index = target_arc * capacity + jnp.sum(earlier.astype(jnp.int32), axis=1)
    slot_rows = (
        jnp.zeros((arc_groups * capacity, maximum_row_count, slice_width), jnp.float32)
        .at[slot_index]
        .set(remaining_columns)
    )
    labels = jnp.full((arc_groups * capacity,), -1, jnp.int32).at[slot_index].set(target_slice)
    arrived, arrived_labels = (
        lax.all_to_all(slot_rows, "arc", split_axis=0, concat_axis=0, tiled=True),
        lax.all_to_all(labels, "arc", split_axis=0, concat_axis=0, tiled=True),
    )
    block_grams = jnp.einsum("nrw,nrv->nwv", arrived, arrived, precision=highest_precision)
    select = (arrived_labels[:, None] == jnp.arange(SLICE_DEV, dtype=jnp.int32)[None, :]).astype(
        jnp.float32
    )
    added = jnp.einsum("ns,nwv->swv", select, block_grams, precision=highest_precision)
    information = (
        jnp.einsum("sij,sik->sjk", prior_factor, prior_factor, precision=highest_precision) + added
    )
    factor_low = jnp.linalg.cholesky(information)
    return jnp.swapaxes(factor_low, 1, 2)


def solution(mesh):
    placed = (
        P(("arc", "col"), None, None),
        P("arc", None, "col"),
        P("arc"),
        P(("arc", "col")),
        P(("arc", "col"), None, None),
    )
    return jax.shard_map(
        per_device,
        mesh=mesh,
        in_specs=placed,
        out_specs=P(("arc", "col"), None, None),
        check_vma=False,
    )
```

profile of v0, /device:TPU:24, one launch (start us, length us, event | category | flops | bytes accessed | tf_op | source)
XLA Modules:
  0.0 603.9 jit_solution(8492487142144638264)
XLA Ops:
  0.0 6.6 %copy.71 = f32[128,320,32]{1,2,0:T(8,128)} copy(f32[128,320,32]{0,2,1:T(8,128)} %param.6) | data formatting | bytes 10485760 | tf_op args[1]
  6.6 5.8 all-to-all-start.1
  12.6 4.3 fusion.8
  19.2 93.8 %custom-call.38 = f32[8,128,128]{2,1,0:T(8,128)S(1)} custom-call(f32[8,128,128]{2,1,0:T(8,128)S(1)} %fusion.14), custom_call_target="Cholesky" | custom-call | tf_op jit(solution)/shard_map/jit(cholesky)/cholesky | solution.py:20
  113.4 79.2 %custom-call.39 = f32[8,1,128,128]{2,3,1,0:T(8,128)} custom-call(f32[8,1,128,128]{3,2,1,0:T(8,128)S(1)} %select_bitcast_fusion.1), custom_call_target="InvertDiagBlocksLowerTriangular" | custom-call | tf_op jit(solution)/shard_map/triangular_solve | solution.py:21
  197.0 7.7 %all-to-all-start = ((s32[8,2,1]{1,2,0:T(1,128)}), s32[8,2,1]{1,2,0:T(1,128)S(1)}, u32[]{:S(2)}, u32[]{:S(2)}) async-start(s32[8,2,1]{1,2,0:T(1,128)} %bitcast), calls=%async_computation | async-start | bytes 8192 | tf_op jit(solution)/shard_map/all_to_all | solution.py:61
  204.7 6.2 %copy.72 = f32[8,320,16,32]{1,3,2,0:T(8,128)} copy(f32[8,320,16,32]{1,3,0,2:T(8,128)} %bitcast.3) | data formatting | bytes 10485760 | tf_op jit(solution)/shard_map/all_to_all | solution.py:42
  210.9 6.3 %copy.73 = f32[8,320,512]{2,1,0:T(8,128)} copy(f32[8,320,512]{1,2,0:T(8,128)} %bitcast.55) | data formatting | bytes 10485760 | tf_op jit(solution)/shard_map/all_to_all | solution.py:42
  217.1 6.7 %fusion.2 = f32[8,128,512]{2,1,0:T(8,128)S(1)} fusion(f32[8,320,128]{2,1,0:T(8,128)S(1)} %fusion.6, f32[8,320,512]{2,1,0:T(8,128)} %copy.73, f32[8,320]{1,0:T(8,128)S(1)} %fusion.25), kind=kOutput, calls=%fused_computation.5 | convolution fusion | flops 2014576640 | bytes 8660992 | tf_op jit(solution)/shard_map/arl,arc->alc/dot_general | solution.py:27
  223.9 6.3 %multiply_subtract_fusion = f32[8,320,512]{2,1,0:T(8,128)} fusion(f32[8,320,512]{2,1,0:T(8,128)S(1)} %copy-done.1, f32[8,320]{1,0:T(8,128)S(1)} %fusion.25, f32[8,320,128]{2,1,0:T(8,128)S(1)} %fusion.6, f32[8,128,512]{2,1,0:T(8,128)S(1)} %fusion.2), kind=kOutput, calls=%fused_computation.4 | convolution fusion | flops 2015887360 | bytes 13903872 | tf_op jit(solution)/shard_map/arl,alc->arc/dot_general | solution.py:28
  230.1 5.3 broadcast_in_dim.14
  235.5 9.1 %scatter_fusion = f32[16,320,512]{2,1,0:T(8,128)} fusion(f32[16,320,512]{2,1,0:T(8,128)} %broadcast_in_dim.14, s32[8]{0:T(128)S(1)} %compare_select_fusion, f32[8,320,512]{2,1,0:T(8,128)} %multiply_subtract_fusion), kind=kCustom, calls=%fused_computation.1 | custom fusion | bytes 15728672 | tf_op jit(solution)/shard_map/scatter | solution.py:56
  244.6 7.4 %all-to-all-start.2 = ((f32[16,320,512]{2,1,0:T(8,128)}), f32[16,320,512]{2,1,0:T(8,128)}, u32[]{:S(2)}, u32[]{:S(2)}) async-start(f32[16,320,512]{2,1,0:T(8,128)} %scatter_fusion), calls=%async_computation.2 | async-start | bytes 20971520 | tf_op jit(solution)/shard_map/all_to_all | solution.py:60
  253.3 114.8 %all-to-all-done.2 = f32[16,320,512]{2,1,0:T(8,128)} async-done(((f32[16,320,512]{2,1,0:T(8,128)}), f32[16,320,512]{2,1,0:T(8,128)}, u32[]{:S(2)}, u32[]{:S(2)}) %all-to-all-start.2) | async-done | bytes 10485792 | tf_op jit(solution)/shard_map/all_to_all | solution.py:60
  368.1 31.2 %fusion.33 = f32[16,512,512]{2,1,0:T(8,128)S(1)} fusion(f32[16,320,512]{2,1,0:T(8,128)} %all-to-all-done.2), kind=kOutput, calls=%fused_computation.80 | convolution fusion | flops 16106127360 | bytes 27262976 | tf_op jit(solution)/shard_map/nrw,nrv->nwv/dot_general | solution.py:63
  399.3 13.9 %fusion = f32[2,512,512]{2,0,1:T(2,128)} fusion(f32[16,512,512]{2,1,0:T(8,128)S(1)} %fusion.33, s32[16]{0:T(128)S(1)} %eq.33), kind=kOutput, calls=%fused_computation.2 | convolution fusion | flops 100663328 | bytes 18874432 | tf_op jit(solution)/shard_map/ns,nwv->swv/dot_general | solution.py:67
  417.4 6.0 convolution_add_fusion
  430.3 23.6 %custom-call.40 = f32[2,128,128]{2,1,0:T(8,128)S(1)} custom-call(f32[2,128,128]{2,1,0:T(8,128)S(1)} %cholesky.314), custom_call_target="Cholesky" | custom-call | tf_op jit(solution)/shard_map/jit(cholesky)/cholesky | solution.py:71
  455.6 19.7 %custom-call.41 = f32[2,1,128,128]{2,3,1,0:T(8,128)S(1)} custom-call(f32[2,1,128,128]{3,2,1,0:T(8,128)S(1)} %select_bitcast_fusion.4), custom_call_target="InvertDiagBlocksLowerTriangular" | custom-call | tf_op jit(solution)/shard_map/jit(cholesky)/cholesky | solution.py:71
  479.0 23.5 %custom-call.42 = f32[2,128,128]{2,1,0:T(8,128)S(1)} custom-call(f32[2,128,128]{2,1,0:T(8,128)S(1)} %cholesky.318), custom_call_target="Cholesky" | custom-call | tf_op jit(solution)/shard_map/jit(cholesky)/cholesky | solution.py:71
  503.2 19.9 %custom-call.43 = f32[2,1,128,128]{2,3,1,0:T(8,128)S(1)} custom-call(f32[2,1,128,128]{3,2,1,0:T(8,128)S(1)} %get-tuple-element.12), custom_call_target="InvertDiagBlocksLowerTriangular" | custom-call | tf_op jit(solution)/shard_map/jit(cholesky)/cholesky | solution.py:71
  526.0 23.5 %custom-call.44 = f32[2,128,128]{2,1,0:T(8,128)S(1)} custom-call(f32[2,128,128]{2,1,0:T(8,128)S(1)} %cholesky.323), custom_call_target="Cholesky" | custom-call | tf_op jit(solution)/shard_map/jit(cholesky)/cholesky | solution.py:71
  550.1 19.7 %custom-call.45 = f32[2,1,128,128]{2,3,1,0:T(8,128)S(1)} custom-call(f32[2,1,128,128]{3,2,1,0:T(8,128)S(1)} %get-tuple-element.10), custom_call_target="InvertDiagBlocksLowerTriangular" | custom-call | tf_op jit(solution)/shard_map/jit(cholesky)/cholesky | solution.py:71
  572.5 23.7 %custom-call.46 = f32[2,128,128]{2,1,0:T(8,128)S(1)} custom-call(f32[2,128,128]{2,1,0:T(8,128)S(1)} %convolution_subtract_fusion.2), custom_call_target="Cholesky" | custom-call | tf_op jit(solution)/shard_map/jit(cholesky)/cholesky | solution.py:71
  (55 shorter events, 39.3 us)
Async XLA Ops:
  0.0 417.4 %copy-start = (f32[2,512,512]{2,1,0:T(8,128)S(1)}, f32[2,512,512]{2,1,0:T(8,128)}, u32[]{:S(2)}) copy-start(f32[2,512,512]{2,1,0:T(8,128)} %param.9) | copy-start | bytes 6291460
  6.6 5.8 copy-start.4
  6.6 5.9 copy-start.3
  6.6 190.3 %all-to-all-start.1 = ((f32[128,320,32]{1,2,0:T(8,128)}), f32[128,320,32]{1,2,0:T(8,128)}, u32[]{:S(2)}, u32[]{:S(2)}) async-start(f32[128,320,32]{1,2,0:T(8,128)} %copy.71), calls=%async_computation.1 | async-start | bytes 12582912 | tf_op jit(solution)/shard_map/all_to_all | solution.py:42
  16.9 175.7 %copy-start.5 = (s32[8]{0:T(128)S(1)}, s32[8]{0:T(128)}, u32[]{:S(2)}) copy-start(s32[8]{0:T(128)} %param.8) | copy-start | bytes 100
  197.0 47.6 %all-to-all-start = ((s32[8,2,1]{1,2,0:T(1,128)}), s32[8,2,1]{1,2,0:T(1,128)S(1)}, u32[]{:S(2)}, u32[]{:S(2)}) async-start(s32[8,2,1]{1,2,0:T(1,128)} %bitcast), calls=%async_computation | async-start | bytes 8192 | tf_op jit(solution)/shard_map/all_to_all | solution.py:61
  217.1 6.8 %copy-start.1 = (f32[8,320,512]{2,1,0:T(8,128)S(1)}, f32[8,320,512]{2,1,0:T(8,128)}, u32[]{:S(2)}) copy-start(f32[8,320,512]{2,1,0:T(8,128)} %copy.73) | copy-start | bytes 15728644
  244.6 123.5 %all-to-all-start.2 = ((f32[16,320,512]{2,1,0:T(8,128)}), f32[16,320,512]{2,1,0:T(8,128)}, u32[]{:S(2)}, u32[]{:S(2)}) async-start(f32[16,320,512]{2,1,0:T(8,128)} %scatter_fusion), calls=%async_computation.2 | async-start | bytes 20971520 | tf_op jit(solution)/shard_map/all_to_all | solution.py:60
  429.0 1.4 copy-start.2
where the time goes:
time: 613 us; the launch traced here: 604 us
  other arithmetic  337 us (55%)
  waiting for transfers between devices  115 us (19%)
  matrix products  80.6 us (13%)
  local copies, waits for them, and re-layouts  49.6 us (8%)
  starting transfers between devices  20.9 us (3%)
    another operation x15, other arithmetic, per_device(): factor_low = jnp.linalg.cholesky(information)  156 us
    all_to_all x1, waiting for transfers between devices, per_device(): lax.all_to_all(slot_rows, 'arc', split_axis=0, concat_axis=0, tiled=True)  115 us
    another operation x3, other arithmetic, orthonormal(): factor_low = jnp.linalg.cholesky(local_gram)  93.9 us
    another operation x3, other arithmetic, orthonormal(): lax.linalg.triangular_solve(factor_low, masked, left_side=False, lower=Tr...  79.4 us
    dot_general x1, matrix products, per_device(): jnp.einsum('nrw,nrv->nwv', arrived, arrived, precision=highest_precision)  31.2 us
    dot_general x1, matrix products, per_device(): jnp.einsum('ns,nwv->swv', select, block_grams, precision=highest_precision)  13.9 us
    all_to_all x2, local copies, waits for them, and re-layouts, per_device(): lax.all_to_all(global_obs, 'col', split_axis=0, concat_axis=2, tiled=True)  12.4 us
  transfers between devices with their start and end apart: 3, of which 1 were waited for; matrix products, arithmetic and copies ran while one was open for 37% of the time, Pallas kernels for 0%

commit v1 on v0

v1 whole, which is shorter than its diff:
```python
import functools

import jax
import jax.numpy as jnp
from jax import lax
from jax.experimental import pallas as pl
from jax.experimental.pallas import tpu as pltpu
from jax.sharding import PartitionSpec as P

SLICE_DEV = 2
CHUNKS = 2
HI = lax.Precision.HIGHEST
F32 = jnp.float32
BF16 = jnp.bfloat16
NN = (((1,), (0,)), ((), ()))
NT = (((1,), (1,)), ((), ()))
TN = (((0,), (0,)), ((), ()))
VMEM_LIMIT = 48 * 1024 * 1024


def dot(a, b, dims, precision=None):
    return lax.dot_general(a, b, dims, precision=precision, preferred_element_type=F32)


def split2(x):
    high = x.astype(BF16)
    return high, (x - high.astype(F32)).astype(BF16)


def dot3(a, b, dims):
    ah, al = a
    bh, bl = b
    return dot(ah, bh, dims) + (dot(ah, bl, dims) + dot(al, bh, dims))


def split3(x):
    high = x.astype(BF16).astype(F32)
    rest = x - high
    mid = rest.astype(BF16).astype(F32)
    return high, mid, rest - mid


def outer6(left, right):
    lh, lm, ll = split3(left)
    rh, rm, rl = split3(right)
    a = jnp.concatenate([lh, lh, lm, lh, ll, lm], axis=0).astype(BF16)
    b = jnp.concatenate([rh, rm, rh, rl, rh, rm], axis=0).astype(BF16)
    return dot(a, b, TN)


def row_of(x, i):
    return jnp.broadcast_to(x[i : i + 1, :], x.shape)


def lane_of(x, i):
    return jnp.broadcast_to(x[:, i : i + 1], x.shape)


def panel_places(p):
    lane = lax.broadcasted_iota(jnp.int32, (8, 128), 1) - 8 * p
    sub = lax.broadcasted_iota(jnp.int32, (8, 128), 0)
    return lane, sub


def cholesky_panel(a_ref, b, p, store_upper):
    lane, sub = panel_places(p)
    x = a_ref[b, pl.ds(pl.multiple_of(8 * p, 8), 8), :]
    d = pltpu.roll(x, lax.rem(128 - 8 * p, 128), 1)
    c = [lane_of(d, l) for l in range(8)]
    m = [(sub == k).astype(F32) for k in range(8)]
    for i in range(8):
        r = lax.rsqrt(row_of(c[i], i))
        unit = (sub == i).astype(F32)
        lm = jnp.where(sub >= i, c[i] * r, 0.0) - unit
        for l in range(i + 1, 8):
            c[l] = c[l] - lm * (row_of(c[l], i) * r)
        for k in range(i + 1):
            m[k] = m[k] - lm * (row_of(m[k], i) * r)
    own = lane == sub
    inside = (lane >= 0) & (lane < 8)
    upper = m[0] * row_of(x, 0)
    for k in range(1, 8):
        upper = upper + m[k] * row_of(x, k)
    place = jnp.where(lane == 0, m[0], upper)
    for k in range(1, 8):
        place = jnp.where(lane == k, m[k], place)
    if store_upper is not None:
        store_upper(jnp.where(lane >= sub, upper, 0.0))
    t = outer6(jnp.where(lane >= 8, upper, 0.0), place)
    rows = lax.broadcasted_iota(jnp.int32, (128, 128), 0)
    lanes = lax.broadcasted_iota(jnp.int32, (128, 128), 1) - 8 * p
    cleared = (lanes >= 0) & (lanes < 8) & (rows >= 8 * p + 8)
    a_ref[b] = jnp.where(cleared, 0.0, a_ref[b]) - t
    a_ref[b, pl.ds(pl.multiple_of(8 * p, 8), 8), :] = place


def inverse_panel(a_ref, sign_ref, b, p):
    lane, sub = panel_places(p)
    x = a_ref[b, pl.ds(pl.multiple_of(8 * p, 8), 8), :]
    d = pltpu.roll(x, lax.rem(128 - 8 * p, 128), 1)
    c = [lane_of(d, l) for l in range(8)]
    m = [(sub == k).astype(F32) for k in range(8)]
    signs = sign_ref[b]
    for i in range(8):
        pv = row_of(c[i], i)
        s = jnp.where(pv >= 0.0, -1.0, 1.0)
        signs = jnp.where(lane == i, s, signs)
        inv = 1.0 / (pv - s)
        lm = jnp.where(sub == i, 1.0 - inv, c[i] * inv)
        for l in range(i + 1, 8):
            c[l] = c[l] - lm * row_of(c[l], i)
        for k in range(i + 1):
            m[k] = m[k] - lm * row_of(m[k], i)
    sign_ref[b] = signs
    place = m[0] * row_of(x, 0)
    for k in range(1, 8):
        place = place + m[k] * row_of(x, k)
    for k in range(8):
        place = jnp.where(lane == k, m[k], place)
    rows = lax.broadcasted_iota(jnp.int32, (128, 128), 0) - 8 * p
    lanes = lax.broadcasted_iota(jnp.int32, (128, 128), 1) - 8 * p
    wide = jnp.concatenate([place] * 16, axis=0)
    factor = jnp.where((rows >= 0) & (rows < 8), wide, 0.0)
    a = a_ref[b]
    t = dot(a, factor, NN, HI)
    a_ref[b] = jnp.where((lanes >= 0) & (lanes < 8), 0.0, a) - t
    a_ref[b, pl.ds(pl.multiple_of(8 * p, 8), 8), :] = place


def layout_kernel(x_ref, o_ref):
    rows, cols, arcs = x_ref.shape
    half = cols // 2
    for j in range(half):
        first = x_ref[:, j, :]
        second = x_ref[:, j + half, :]
        for tile in range(2):
            o_ref[:, tile * cols + j, :] = first[tile * 128 : tile * 128 + 128].T
            o_ref[:, tile * cols + j + half, :] = second[tile * 128 : tile * 128 + 128].T
        o_ref[:, 2 * cols + j, :] = jnp.concatenate([first[256:], second[256:]], axis=0).T


def layout(x, chunk):
    rows, cols, arcs = x.shape
    part = cols // CHUNKS
    packed = 2 * part + part // 2
    return pl.pallas_call(
        layout_kernel,
        out_shape=jax.ShapeDtypeStruct((arcs, packed, 128), F32),
        grid=(1,),
        in_specs=[pl.BlockSpec((rows, part, arcs), lambda i: (0, chunk, 0))],
        out_specs=pl.BlockSpec((arcs, packed, 128), lambda i: (0, 0, 0)),
        compiler_params=pltpu.CompilerParams(vmem_limit_bytes=VMEM_LIMIT),
    )(x)


def local_kernel(counts_ref, l_ref, z_ref, a_ref, q_ref, sign_ref):
    arcs, rows, loc = l_ref.shape
    place = lax.broadcasted_iota(jnp.int32, (rows, loc), 0)
    for b in range(arcs):
        masked = jnp.where(place < counts_ref[b], l_ref[b], 0.0)
        q_ref[b] = masked
        a_ref[b] = dot(masked, masked, TN, HI)

    def factor(p, carry):
        for b in range(arcs):
            cholesky_panel(a_ref, b, p, None)
        return carry

    lax.fori_loop(0, loc // 8, factor, 0)
    r = lax.broadcasted_iota(jnp.int32, (loc, loc), 0)
    l = lax.broadcasted_iota(jnp.int32, (loc, loc), 1)
    for b in range(arcs):
        basis = dot(q_ref[b], jnp.where(l <= r, a_ref[b], 0.0), NT, HI)
        q_ref[b] = basis
        a_ref[b] = basis[:loc]
    sign_ref[...] = jnp.zeros_like(sign_ref)

    def invert(p, carry):
        for b in range(arcs):
            inverse_panel(a_ref, sign_ref, b, p)
        return carry

    lax.fori_loop(0, loc // 8, invert, 0)
    rest = rows - loc
    unit = (place == lax.broadcasted_iota(jnp.int32, (rows, loc), 1)).astype(F32)
    r2 = lax.broadcasted_iota(jnp.int32, (rest, rows), 0)
    l2 = lax.broadcasted_iota(jnp.int32, (rest, rows), 1)
    for b in range(arcs):
        q = q_ref[b]
        n = dot(q[loc:], a_ref[b], NN, HI)
        v = q * sign_ref[b][0:1] - unit
        keep = (l2 == r2 + loc) & (l2 < counts_ref[b])
        z = dot(n, v, NT, HI) + keep.astype(F32)
        tail = z[:, 256:]
        gap = jnp.zeros_like(tail)
        wide = jnp.concatenate([z[:, :256], tail, gap, gap, tail], axis=1)
        blank = jnp.zeros((64, wide.shape[1]), F32)
        tall = jnp.concatenate([wide[:loc], blank, wide[loc:], blank], axis=0)
        zh, zl = split2(tall)
        z_ref[b, 0] = zh
        z_ref[b, 1] = zl


def local_part(counts, local_obs):
    arcs, rows, loc = local_obs.shape
    return pl.pallas_call(
        local_kernel,
        out_shape=jax.ShapeDtypeStruct((arcs, 2, rows, 512), BF16),
        in_specs=[pl.BlockSpec(memory_space=pltpu.SMEM), pl.BlockSpec(memory_space=pltpu.VMEM)],
        out_specs=pl.BlockSpec(memory_space=pltpu.VMEM),
        scratch_shapes=[
            pltpu.VMEM((arcs, loc, loc), F32),
            pltpu.VMEM((arcs, rows, loc), F32),
            pltpu.VMEM((arcs, 8, loc), F32),
        ],
        compiler_params=pltpu.CompilerParams(vmem_limit_bytes=VMEM_LIMIT),
    )(counts, local_obs)


def eliminate_kernel(dest_ref, slot_ref, g_ref, z_ref, o_ref):
    sources, arcs, packed, _ = g_ref.shape
    part = packed * 2 // 5
    half = part // 2
    width = sources * part
    o_ref[...] = jnp.zeros_like(o_ref)

    def arc(a, carry):
        slot = slot_ref[a]
        dest = dest_ref[a]
        tails = pl.ds(pl.multiple_of(192 - 64 * slot, 64), 128)
        z = [jnp.concatenate([z_ref[a, i, :128, :], z_ref[a, i, tails, :]], axis=0) for i in range(2)]
        g = [g_ref[:, a, i * part : (i + 1) * part, :].reshape(width, 128) for i in range(2)]
        t = split2(g_ref[:, a, 2 * part :, :].reshape(width // 2, 128))
        body = dot3(split2(jnp.concatenate(g, axis=1)), [w[:, :256] for w in z], NT)
        ends = [dot3(t, [w[:, 256 + 128 * i : 384 + 128 * i] for w in z], NT) for i in range(2)]
        ends = jnp.stack([e.reshape(sources, half, 256) for e in ends], axis=1).reshape(width, 256)
        r = body + ends
        o_ref[dest, :, pl.ds(pl.multiple_of(256 * slot, 128), 128)] = r[:, :128]
        o_ref[dest, :, 128:256] = o_ref[dest, :, 128:256] + r[:, 128:]
        return carry

    lax.fori_loop(0, arcs, arc, 0)


def eliminate(dest, slot, g, z, groups):
    sources, arcs, packed, _ = g.shape
    width = sources * packed * 2 // 5
    smem = pl.BlockSpec(memory_space=pltpu.SMEM)
    vmem = pl.BlockSpec(memory_space=pltpu.VMEM)
    return pl.pallas_call(
        eliminate_kernel,
        out_shape=jax.ShapeDtypeStruct((groups, width, 384), F32),
        in_specs=[smem, smem, vmem, vmem],
        out_specs=vmem,
        compiler_params=pltpu.CompilerParams(vmem_limit_bytes=VMEM_LIMIT),
    )(dest, slot, g, z)


def factor_kernel(part, labels_ref, *refs):
    arrived = refs[:CHUNKS]
    prior_ref, out_ref, info_ref, high_ref, low_ref, a_ref = refs[CHUNKS:]
    slices, width, _ = prior_ref.shape
    groups = arrived[0].shape[0]
    half = width // 2
    info_ref[...] = prior_ref[...]
    lane = lax.broadcasted_iota(jnp.int32, (width, 384), 1)

    def add(n, carry):
        first, second = labels_ref[2 * n], labels_ref[2 * n + 1]
        pieces = [a[n].reshape(width // (CHUNKS * part), 1, part, 384) for a in arrived]
        x = jnp.concatenate(pieces, axis=1).reshape(width, 384)
        xh, xl = split2(x)
        high_ref[...] = xh
        low_ref[...] = xl
        for s in range(slices):

            @pl.when((first == s) | (second == s))
            def _():
                own = jnp.where(lane < 192, first, second) == s
                h, l = high_ref[...], low_ref[...]
                mh = jnp.where(own, h, jnp.zeros_like(h))
                ml = jnp.where(own, l, jnp.zeros_like(l))
                info_ref[s, :half] += dot3((mh[:half], ml[:half]), (h, l), NT)
                info_ref[s, half:, half:] += dot3((mh[half:], ml[half:]), (h[half:], l[half:]), NT)

        return carry

    lax.fori_loop(0, groups, add, 0)
    r = lax.broadcasted_iota(jnp.int32, (128, 128), 0)
    l = lax.broadcasted_iota(jnp.int32, (128, 128), 1)
    for k in range(width // 128):
        lo, hi = 128 * k, 128 * k + 128
        for s in range(slices):
            a_ref[s] = info_ref[s, lo:hi, lo:hi]
            if k:
                out_ref[s, lo:hi, :lo] = jnp.zeros((128, lo), F32)

        def step(p, carry):
            for s in range(slices):

                def store(rows):
                    out_ref[s, pl.ds(pl.multiple_of(lo + 8 * p, 8), 8), lo:hi] = rows

                cholesky_panel(a_ref, s, p, store)
            return carry

        lax.fori_loop(0, 16, step, 0)
        if hi < width:
            for s in range(slices):
                inverse = jnp.where(l <= r, a_ref[s], 0.0)
                u = dot(inverse, info_ref[s, lo:hi, hi:], NN, HI)
                out_ref[s, lo:hi, hi:] = u
                for j in range(hi, width, 128):
                    info_ref[s, j : j + 128, j:] -= dot(u[:, j - hi : j - hi + 128], u[:, j - hi :], TN, HI)


def factor(part, labels, arrived, prior_gram):
    slices, width, _ = prior_gram.shape
    vmem = pl.BlockSpec(memory_space=pltpu.VMEM)
    return pl.pallas_call(
        functools.partial(factor_kernel, part),
        out_shape=jax.ShapeDtypeStruct(prior_gram.shape, F32),
        in_specs=[pl.BlockSpec(memory_space=pltpu.SMEM)] + [vmem] * (CHUNKS + 1),
        out_specs=vmem,
        scratch_shapes=[
            pltpu.VMEM((slices, width, width), F32),
            pltpu.VMEM((width, 384), BF16),
            pltpu.VMEM((width, 384), BF16),
            pltpu.VMEM((slices, 128, 128), F32),
        ],
        compiler_params=pltpu.CompilerParams(vmem_limit_bytes=VMEM_LIMIT),
    )(labels, *arrived, prior_gram)


def slots_of(owner, col_groups):
    dest = owner // SLICE_DEV // col_groups
    order = jnp.arange(owner.shape[-1], dtype=jnp.int32)
    earlier = (dest[..., None, :] == dest[..., :, None]) & (order[None, :] < order[:, None])
    return dest, jnp.sum(earlier.astype(jnp.int32), axis=-1), owner % SLICE_DEV


def per_device(local_obs, global_obs, row_counts, owner_map, prior_factor):
    arc_dev = local_obs.shape[0]
    arc_groups = lax.axis_size("arc")
    col_groups = lax.axis_size("col")
    part = global_obs.shape[2] // CHUNKS
    counts = lax.dynamic_slice_in_dim(row_counts, lax.axis_index("col") * arc_dev, arc_dev)
    x = jnp.transpose(global_obs, (1, 2, 0))
    columns = []
    for h in range(CHUNKS):
        packed = layout(x, h)
        moved = lax.all_to_all(packed, "col", split_axis=0, concat_axis=0, tiled=True)
        columns.append(moved.reshape(col_groups, arc_dev, *moved.shape[1:]))
    owners = lax.all_gather(owner_map, "arc", axis=0)
    dest, slot, label = slots_of(owners, col_groups)
    mine = (dest == lax.axis_index("arc"))[:, :, None] & (slot[:, :, None] == jnp.arange(2, dtype=jnp.int32))
    labels = (jnp.sum(jnp.where(mine, label[:, :, None] + 1, 0), axis=1) - 1).reshape(-1)
    own_dest, own_slot, _ = slots_of(owner_map, col_groups)
    z = local_part(counts, local_obs)
    prior_gram = jnp.einsum("sij,sik->sjk", prior_factor, prior_factor, precision=HI)
    arrived = []
    for h in range(CHUNKS):
        kept = eliminate(own_dest, own_slot, columns[h], z, arc_groups)
        arrived.append(lax.all_to_all(kept, "arc", split_axis=0, concat_axis=0, tiled=True))
    return factor(part, labels, arrived, prior_gram)


def solution(mesh):
    placed = (
        P(("arc", "col"), None, None),
        P("arc", None, "col"),
        P("arc"),
        P(("arc", "col")),
        P(("arc", "col"), None, None),
    )
    return jax.shard_map(
        per_device,
        mesh=mesh,
        in_specs=placed,
        out_specs=P(("arc", "col"), None, None),
        check_vma=False,
    )
```

time: 613 us -> 373 us (0.61)
  other arithmetic: 337 us -> 0.67 us
  Pallas kernels: 0 us -> 226 us
  matrix products: 80.6 us -> 4.85 us
  waiting for transfers between devices: 115 us -> 61.3 us
  blocking collectives: 0 us -> 43.7 us
  local copies, waits for them, and re-layouts: 49.6 us -> 9.2 us
    another operation x21 -> x0, other arithmetic: 329 us -> none  [the longest x15 156 us: per_device(): factor_low = jnp.linalg.cholesky(information)]
    pallas_call x0 -> x6, Pallas kernels: none -> 226 us  [the longest x1 133 us: local_part(): pl.pallas_call(local_kernel, out_shape=jax.ShapeDtypeStruct((arcs, 2, row...]
    dot_general x6 -> x1, matrix products: 68.4 us -> 4.85 us  [per_device(): jnp.einsum('sij,sik->sjk', prior_factor, prior_factor, precision=HI)]
    all_to_all x3 -> x4, waiting for transfers between devices: 115 us -> 61.3 us  [the longest x2 31.8 us: per_device(): lax.all_to_all(packed, 'col', split_axis=0, concat_axis=0, tiled=True)]
    unnamed x0 -> x1, blocking collectives: none -> 43.7 us
    all_to_all x4 -> x0, local copies, waits for them, and re-layouts: 13.6 us -> none  [the longest x2 12.4 us: per_device(): lax.all_to_all(global_obs, 'col', split_axis=0, concat_axis=2, tiled=True)]
    another operation x7 -> x0, matrix products: 12.2 us -> none  [the longest x6 9.39 us: per_device(): factor_low = jnp.linalg.cholesky(information)]
    scatter x2 -> x0, local copies, waits for them, and re-layouts: 9.69 us -> none  [the longest x1 9.09 us: per_device(): slot_rows = jnp.zeros((arc_groups * capacity, maximum_row_count, slice_wi...]
  transfers between devices with their start and end apart: 3 -> 4, of which waited for: 1 -> 2; matrix products, arithmetic and copies ran while one was open for 37% -> 2% of each run, Pallas kernels for 0% -> 41%
where the time goes in v1:
time: 373 us; the launch traced here: 370 us
  Pallas kernels  226 us (61%)
  waiting for transfers between devices  61.3 us (16%)
  blocking collectives  43.7 us (12%)
  starting transfers between devices  22.7 us (6%)
  local copies, waits for them, and re-layouts  9.2 us (2%)
  matrix products  4.85 us (1%)
    pallas_call x1, Pallas kernels, local_part(): pl.pallas_call(local_kernel, out_shape=jax.ShapeDtypeStruct((arcs, 2, row...  133 us
    pallas_call x1, Pallas kernels, factor(): pl.pallas_call(functools.partial(factor_kernel, part), out_shape=jax.Shap...  71.1 us
    unnamed x1, blocking collectives  43.7 us
    all_to_all x2, waiting for transfers between devices, per_device(): lax.all_to_all(packed, 'col', split_axis=0, concat_axis=0, tiled=True)  31.8 us
    all_to_all x2, waiting for transfers between devices, per_device(): lax.all_to_all(kept, 'arc', split_axis=0, concat_axis=0, tiled=True)  29.6 us
    pallas_call x2, Pallas kernels, eliminate(): pl.pallas_call(eliminate_kernel, out_shape=jax.ShapeDtypeStruct((groups,...  13.6 us
    all_to_all x2, starting transfers between devices, per_device(): lax.all_to_all(kept, 'arc', split_axis=0, concat_axis=0, tiled=True)  12.2 us
    all_to_all x2, starting transfers between devices, per_device(): lax.all_to_all(packed, 'col', split_axis=0, concat_axis=0, tiled=True)  10.5 us
  transfers between devices with their start and end apart: 4, of which 2 were waited for; matrix products, arithmetic and copies ran while one was open for 2% of the time, Pallas kernels for 41%

profile of v1, /device:TPU:24, one launch (start us, length us, event | category | flops | bytes accessed | tf_op | source)
XLA Modules:
  0.0 369.6 jit_solution(7577425017002613755)
XLA Ops:
  0.0 4.6 %shard_map.55 = f32[128,40,128]{2,1,0:T(8,128)S(1)} custom-call(f32[320,32,128]{2,1,0:T(8,128)} %bitcast.6), custom_call_target="tpu_custom_call" | custom-call | tf_op jit(solution)/shard_map/pallas_call | solution.py:146
  4.6 1.5 copy-done.4
  6.2 5.6 %all-to-all-start = ((f32[128,40,128]{2,1,0:T(8,128)}), f32[128,40,128]{2,1,0:T(8,128)}, u32[]{:S(2)}, u32[]{:S(2)}) async-start(f32[128,40,128]{2,1,0:T(8,128)} %copy-done.4), calls=%async_computation | async-start | bytes 5242880 | tf_op jit(solution)/shard_map/all_to_all | solution.py:352
  11.8 4.5 %shard_map.58 = f32[128,40,128]{2,1,0:T(8,128)S(1)} custom-call(f32[320,32,128]{2,1,0:T(8,128)} %bitcast.7), custom_call_target="tpu_custom_call" | custom-call | tf_op jit(solution)/shard_map/pallas_call | solution.py:146
  16.3 1.5 copy-done.3
  17.8 31.8 %all-to-all-done = f32[128,40,128]{2,1,0:T(8,128)} async-done(((f32[128,40,128]{2,1,0:T(8,128)}), f32[128,40,128]{2,1,0:T(8,128)}, u32[]{:S(2)}, u32[]{:S(2)}) %all-to-all-start) | async-done | bytes 2621472 | tf_op jit(solution)/shard_map/all_to_all | solution.py:352
  49.5 4.9 %all-to-all-start.2 = ((f32[128,40,128]{2,1,0:T(8,128)}), f32[128,40,128]{2,1,0:T(8,128)}, u32[]{:S(2)}, u32[]{:S(2)}) async-start(f32[128,40,128]{2,1,0:T(8,128)} %copy-done.3), calls=%async_computation.2 | async-start | bytes 5242880 | tf_op jit(solution)/shard_map/all_to_all | solution.py:352
  54.5 132.6 %shard_map.56.z_ref = bf16[8,2,320,512]{3,2,1,0:T(8,128)(2,1)} custom-call(s32[8]{0:T(128)S(1)} %dynamic_slice.3.counts_ref, f32[8,320,128]{2,1,0:T(8,128)S(1)} %copy-done.6), custom_call_target="tpu_custom_call" | custom-call | tf_op jit(solution)/shard_map/pallas_call | solution.py:206
  187.1 0.2 convert_reduce_fusion.1.slot_ref
  187.2 6.8 %shard_map.57 = f32[8,256,384]{2,1,0:T(8,128)S(1)} custom-call(s32[8]{0:T(128)S(1)} %and_select_fusion.dest_ref, s32[8]{0:T(128)S(1)} %convert_reduce_fusion.1.slot_ref, f32[16,8,40,128]{3,2,1,0:T(8,128)} %bitcast.2.g_ref, bf16[8,2,320,512]{3,2,1,0:T(8,128)(2,1)} %shard_map.56.z_ref), custom_call_target="tpu_custom_call" | custom-call | tf_op jit(solution)/shard_map/pallas_call | solution.py:250
  194.0 1.7 copy-done.2
  195.8 7.5 %all-to-all-start.1 = ((f32[8,256,384]{2,1,0:T(8,128)}), f32[8,256,384]{2,1,0:T(8,128)}, u32[]{:S(2)}, u32[]{:S(2)}) async-start(f32[8,256,384]{2,1,0:T(8,128)} %copy-done.2), calls=%async_computation.1 | async-start | bytes 6291456 | tf_op jit(solution)/shard_map/all_to_all | solution.py:364
  203.2 6.8 %shard_map.59 = f32[8,256,384]{2,1,0:T(8,128)S(1)} custom-call(s32[8]{0:T(128)S(1)} %and_select_fusion.dest_ref, s32[8]{0:T(128)S(1)} %convert_reduce_fusion.1.slot_ref, f32[16,8,40,128]{3,2,1,0:T(8,128)} %bitcast.3.g_ref, bf16[8,2,320,512]{3,2,1,0:T(8,128)(2,1)} %shard_map.56.z_ref), custom_call_target="tpu_custom_call" | custom-call | tf_op jit(solution)/shard_map/pallas_call | solution.py:250
  210.0 1.7 copy-done.1
  211.8 29.6 %all-to-all-done.1.refs_0_ = f32[8,256,384]{2,1,0:T(8,128)} async-done(((f32[8,256,384]{2,1,0:T(8,128)}), f32[8,256,384]{2,1,0:T(8,128)}, u32[]{:S(2)}, u32[]{:S(2)}) %all-to-all-start.1) | async-done | bytes 3145760 | tf_op jit(solution)/shard_map/all_to_all | solution.py:364
  241.3 4.8 %all-to-all-start.3 = ((f32[8,256,384]{2,1,0:T(8,128)}), f32[8,256,384]{2,1,0:T(8,128)}, u32[]{:S(2)}, u32[]{:S(2)}) async-start(f32[8,256,384]{2,1,0:T(8,128)} %copy-done.1), calls=%async_computation.3 | async-start | bytes 6291456 | tf_op jit(solution)/shard_map/all_to_all | solution.py:364
  246.1 0.6 dynamic-slice
  247.3 0.2 dynamic-update-slice
  247.6 43.7 %all-reduce = s32[64]{0:T(128)S(1)} all-reduce(s32[64]{0:T(128)S(1)} %dynamic-update-slice), channel_id=2, replica_groups=mesh['arc'=8,'col'=16] {'arc'}, use_global_device_ids=true, to_apply=%add | all-reduce | flops 64 | bytes 512
  291.3 0.3 convert_reduce_fusion
  291.6 0.1 select_reduce_fusion
  292.0 4.9 %fusion.6.refs_2_ = f32[2,512,512]{2,1,0:T(8,128)} fusion(f32[2,512,512]{2,1,0:T(8,128)S(1)} %copy-done), kind=kOutput, calls=%fused_computation.32 | convolution fusion | flops 3221225472 | bytes 4194304 | tf_op jit(solution)/shard_map/sij,sik->sjk/dot_general | solution.py:360
  296.8 1.6 copy-done.5
  298.4 71.1 %shard_map.60 = f32[2,512,512]{2,1,0:T(8,128)} custom-call(s32[16]{0:T(128)S(1)} %sub.25.labels_ref, f32[8,256,384]{2,1,0:T(8,128)} %all-to-all-done.1.refs_0_, f32[8,256,384]{2,1,0:T(8,128)} %all-to-all-done.3.refs_1_, f32[2,512,512]{2,1,0:T(8,128)S(1)} %copy-done.5), custom_call_target="tpu_custom_call" | custom-call | tf_op jit(solution)/shard_map/pallas_call | solution.py:320
  (27 shorter events, 0.4 us)
Async XLA Ops:
  0.0 292.0 %copy-start = (f32[2,512,512]{2,1,0:T(8,128)S(1)}, f32[2,512,512]{2,1,0:T(8,128)}, u32[]{:S(2)}) copy-start(f32[2,512,512]{2,1,0:T(8,128)} %param.9) | copy-start | bytes 6291460
  4.6 1.5 copy-start.4
  6.2 43.4 %all-to-all-start = ((f32[128,40,128]{2,1,0:T(8,128)}), f32[128,40,128]{2,1,0:T(8,128)}, u32[]{:S(2)}, u32[]{:S(2)}) async-start(f32[128,40,128]{2,1,0:T(8,128)} %copy-done.4), calls=%async_computation | async-start | bytes 5242880 | tf_op jit(solution)/shard_map/all_to_all | solution.py:352
  16.3 1.5 copy-start.3
  17.8 36.6 %copy-start.7 = (s32[128]{0:T(128)S(1)}, s32[128]{0:T(128)}, u32[]{:S(2)}) copy-start(s32[128]{0:T(128)} %param.7) | copy-start | bytes 1540
  17.8 36.7 %copy-start.6 = (f32[8,320,128]{2,1,0:T(8,128)S(1)}, f32[8,320,128]{2,1,0:T(8,128)}, u32[]{:S(2)}) copy-start(f32[8,320,128]{2,1,0:T(8,128)} %l_ref.1) | copy-start | bytes 3932164
  49.5 146.2 %all-to-all-start.2 = ((f32[128,40,128]{2,1,0:T(8,128)}), f32[128,40,128]{2,1,0:T(8,128)}, u32[]{:S(2)}, u32[]{:S(2)}) async-start(f32[128,40,128]{2,1,0:T(8,128)} %copy-done.3), calls=%async_computation.2 | async-start | bytes 5242880 | tf_op jit(solution)/shard_map/all_to_all | solution.py:352
  54.5 132.6 %copy-start.8 = (s32[8]{0:T(128)S(1)}, s32[8]{0:T(128)}, u32[]{:S(2)}) copy-start(s32[8]{0:T(128)} %param.8) | copy-start | bytes 100
  194.0 1.7 copy-start.2
  195.8 45.5 %all-to-all-start.1 = ((f32[8,256,384]{2,1,0:T(8,128)}), f32[8,256,384]{2,1,0:T(8,128)}, u32[]{:S(2)}, u32[]{:S(2)}) async-start(f32[8,256,384]{2,1,0:T(8,128)} %copy-done.2), calls=%async_computation.1 | async-start | bytes 6291456 | tf_op jit(solution)/shard_map/all_to_all | solution.py:364
  210.0 1.7 copy-start.1
  211.8 34.3 %copy-start.9 = (u32[128]{0:T(128)S(1)}, u32[128]{0:T(128)}, u32[]{:S(2)}) copy-start(u32[128]{0:T(128)} %constant.75) | copy-start | bytes 1540
  241.3 55.5 %all-to-all-start.3 = ((f32[8,256,384]{2,1,0:T(8,128)}), f32[8,256,384]{2,1,0:T(8,128)}, u32[]{:S(2)}, u32[]{:S(2)}) async-start(f32[8,256,384]{2,1,0:T(8,128)} %copy-done.1), calls=%async_computation.3 | async-start | bytes 6291456 | tf_op jit(solution)/shard_map/all_to_all | solution.py:364
  296.8 1.6 copy-start.5

commit v2 on v1

--- a/solution.py
+++ b/solution.py
@@ -8,7 +8,8 @@
 from jax.sharding import PartitionSpec as P
 
 SLICE_DEV = 2
-CHUNKS = 2
+CHUNKS = 1
+GROUP = 8
 HI = lax.Precision.HIGHEST
 F32 = jnp.float32
 BF16 = jnp.bfloat16
@@ -49,58 +50,59 @@
 
 
 def row_of(x, i):
-    return jnp.broadcast_to(x[i : i + 1, :], x.shape)
+    return jnp.broadcast_to(x[:, i : i + 1, :], x.shape)
 
 
 def lane_of(x, i):
-    return jnp.broadcast_to(x[:, i : i + 1], x.shape)
-
-
-def panel_places(p):
-    lane = lax.broadcasted_iota(jnp.int32, (8, 128), 1) - 8 * p
-    sub = lax.broadcasted_iota(jnp.int32, (8, 128), 0)
-    return lane, sub
-
-
-def cholesky_panel(a_ref, b, p, store_upper):
-    lane, sub = panel_places(p)
-    x = a_ref[b, pl.ds(pl.multiple_of(8 * p, 8), 8), :]
-    d = pltpu.roll(x, lax.rem(128 - 8 * p, 128), 1)
-    c = [lane_of(d, l) for l in range(8)]
+    return jnp.broadcast_to(x[:, :, i : i + 1], x.shape)
+
+
+def panel_of(a_ref, which, p):
+    rows = pl.ds(pl.multiple_of(8 * p, 8), 8)
+    x = a_ref[which, rows, :]
+    lane = lax.broadcasted_iota(jnp.int32, x.shape, 2) - 8 * p
+    sub = lax.broadcasted_iota(jnp.int32, x.shape, 1)
+    turned = pltpu.roll(x, lax.rem(128 - 8 * p, 128), 2)
+    c = [lane_of(turned, l) for l in range(8)]
     m = [(sub == k).astype(F32) for k in range(8)]
+    return rows, x, lane, sub, c, m
+
+
+def apply_panel(m, x):
+    terms = [m[k] * row_of(x, k) for k in range(8)]
+    while len(terms) > 1:
+        terms = [terms[i] + terms[i + 1] for i in range(0, len(terms), 2)]
+    return terms[0]
+
+
+def cholesky_panel(a_ref, which, p, store_upper):
+    rows, x, lane, sub, c, m = panel_of(a_ref, which, p)
     for i in range(8):
         r = lax.rsqrt(row_of(c[i], i))
-        unit = (sub == i).astype(F32)
-        lm = jnp.where(sub >= i, c[i] * r, 0.0) - unit
+        lm = jnp.where(sub >= i, c[i] * r, 0.0) - (sub == i).astype(F32)
         for l in range(i + 1, 8):
             c[l] = c[l] - lm * (row_of(c[l], i) * r)
         for k in range(i + 1):
             m[k] = m[k] - lm * (row_of(m[k], i) * r)
-    own = lane == sub
-    inside = (lane >= 0) & (lane < 8)
-    upper = m[0] * row_of(x, 0)
-    for k in range(1, 8):
-        upper = upper + m[k] * row_of(x, k)
-    place = jnp.where(lane == 0, m[0], upper)
-    for k in range(1, 8):
+    upper = apply_panel(m, x)
+    place = upper
+    for k in range(8):
         place = jnp.where(lane == k, m[k], place)
     if store_upper is not None:
         store_upper(jnp.where(lane >= sub, upper, 0.0))
-    t = outer6(jnp.where(lane >= 8, upper, 0.0), place)
-    rows = lax.broadcasted_iota(jnp.int32, (128, 128), 0)
-    lanes = lax.broadcasted_iota(jnp.int32, (128, 128), 1) - 8 * p
-    cleared = (lanes >= 0) & (lanes < 8) & (rows >= 8 * p + 8)
-    a_ref[b] = jnp.where(cleared, 0.0, a_ref[b]) - t
-    a_ref[b, pl.ds(pl.multiple_of(8 * p, 8), 8), :] = place
-
-
-def inverse_panel(a_ref, sign_ref, b, p):
-    lane, sub = panel_places(p)
-    x = a_ref[b, pl.ds(pl.multiple_of(8 * p, 8), 8), :]
-    d = pltpu.roll(x, lax.rem(128 - 8 * p, 128), 1)
-    c = [lane_of(d, l) for l in range(8)]
-    m = [(sub == k).astype(F32) for k in range(8)]
-    signs = sign_ref[b]
+    left = jnp.where(lane >= 8, upper, 0.0)
+    t = jnp.stack([outer6(left[b], place[b]) for b in range(x.shape[0])], axis=0)
+    a = a_ref[which]
+    at_row = lax.broadcasted_iota(jnp.int32, a.shape, 1)
+    at_lane = lax.broadcasted_iota(jnp.int32, a.shape, 2) - 8 * p
+    cleared = (at_lane >= 0) & (at_lane < 8) & (at_row >= 8 * p + 8)
+    a_ref[which] = jnp.where(cleared, 0.0, a) - t
+    a_ref[which, rows, :] = place
+
+
+def inverse_panel(a_ref, sign_ref, which, p):
+    rows, x, lane, sub, c, m = panel_of(a_ref, which, p)
+    signs = sign_ref[which]
     for i in range(8):
         pv = row_of(c[i], i)
         s = jnp.where(pv >= 0.0, -1.0, 1.0)
@@ -111,20 +113,18 @@
             c[l] = c[l] - lm * row_of(c[l], i)
         for k in range(i + 1):
             m[k] = m[k] - lm * row_of(m[k], i)
-    sign_ref[b] = signs
-    place = m[0] * row_of(x, 0)
-    for k in range(1, 8):
-        place = place + m[k] * row_of(x, k)
+    sign_ref[which] = signs
+    place = apply_panel(m, x)
     for k in range(8):
         place = jnp.where(lane == k, m[k], place)
-    rows = lax.broadcasted_iota(jnp.int32, (128, 128), 0) - 8 * p
-    lanes = lax.broadcasted_iota(jnp.int32, (128, 128), 1) - 8 * p
-    wide = jnp.concatenate([place] * 16, axis=0)
-    factor = jnp.where((rows >= 0) & (rows < 8), wide, 0.0)
-    a = a_ref[b]
-    t = dot(a, factor, NN, HI)
-    a_ref[b] = jnp.where((lanes >= 0) & (lanes < 8), 0.0, a) - t
-    a_ref[b, pl.ds(pl.multiple_of(8 * p, 8), 8), :] = place
+    a = a_ref[which]
+    at_row = lax.broadcasted_iota(jnp.int32, a.shape, 1) - 8 * p
+    at_lane = lax.broadcasted_iota(jnp.int32, a.shape, 2) - 8 * p
+    wide = jnp.concatenate([place] * 16, axis=1)
+    factor = jnp.where((at_row >= 0) & (at_row < 8), wide, 0.0)
+    t = jnp.stack([dot(a[b], factor[b], NN, HI) for b in range(x.shape[0])], axis=0)
+    a_ref[which] = jnp.where((at_lane >= 0) & (at_lane < 8), 0.0, a) - t
+    a_ref[which, rows, :] = place
 
 
 def layout_kernel(x_ref, o_ref):
@@ -162,8 +162,8 @@
         a_ref[b] = dot(masked, masked, TN, HI)
 
     def factor(p, carry):
-        for b in range(arcs):
-            cholesky_panel(a_ref, b, p, None)
+        for b in range(0, arcs, GROUP):
+            cholesky_panel(a_ref, slice(b, b + GROUP), p, None)
         return carry
 
     lax.fori_loop(0, loc // 8, factor, 0)
@@ -176,8 +176,8 @@
     sign_ref[...] = jnp.zeros_like(sign_ref)
 
     def invert(p, carry):
-        for b in range(arcs):
-            inverse_panel(a_ref, sign_ref, b, p)
+        for b in range(0, arcs, GROUP):
+            inverse_panel(a_ref, sign_ref, slice(b, b + GROUP), p)
         return carry
 
     lax.fori_loop(0, loc // 8, invert, 0)
@@ -296,12 +296,10 @@
                 out_ref[s, lo:hi, :lo] = jnp.zeros((128, lo), F32)
 
         def step(p, carry):
-            for s in range(slices):
-
-                def store(rows):
-                    out_ref[s, pl.ds(pl.multiple_of(lo + 8 * p, 8), 8), lo:hi] = rows
-
-                cholesky_panel(a_ref, s, p, store)
+            def store(rows):
+                out_ref[:, pl.ds(pl.multiple_of(lo + 8 * p, 8), 8), lo:hi] = rows
+
+            cholesky_panel(a_ref, slice(0, slices), p, store)
             return carry
 
         lax.fori_loop(0, 16, step, 0)

time: 373 us -> 246 us (0.66)
  Pallas kernels: 226 us -> 105 us
  blocking collectives: 43.7 us -> 77.7 us
  waiting for transfers between devices: 61.3 us -> 37.7 us
  starting transfers between devices: 22.7 us -> 13.4 us
  local copies, waits for them, and re-layouts: 9.2 us -> 5.06 us
    pallas_call x1, Pallas kernels: 133 us -> 40.1 us  [local_part(): pl.pallas_call(local_kernel, out_shape=jax.ShapeDtypeStruct((arcs, 2, row...]
    unnamed x1, blocking collectives: 43.7 us -> 77.7 us
    all_to_all x2 -> x1, waiting for transfers between devices: 29.6 us -> 0.01 us  [per_device(): lax.all_to_all(kept, 'arc', split_axis=0, concat_axis=0, tiled=True)]
    pallas_call x1, Pallas kernels: 71.1 us -> 44.3 us  [factor(): pl.pallas_call(functools.partial(factor_kernel, part), out_shape=jax.Shap...]
    all_to_all x2 -> x1, waiting for transfers between devices: 31.8 us -> 37.7 us  [per_device(): lax.all_to_all(packed, 'col', split_axis=0, concat_axis=0, tiled=True)]
    all_to_all x2 -> x1, starting transfers between devices: 10.5 us -> 5.77 us  [per_device(): lax.all_to_all(packed, 'col', split_axis=0, concat_axis=0, tiled=True)]
    all_to_all x2 -> x1, starting transfers between devices: 12.2 us -> 7.61 us  [per_device(): lax.all_to_all(kept, 'arc', split_axis=0, concat_axis=0, tiled=True)]
    unnamed x23 -> x17, local copies, waits for them, and re-layouts: 8.88 us -> 4.74 us
  transfers between devices with their start and end apart: 4 -> 2, of which waited for: 2 -> 1; matrix products, arithmetic and copies ran while one was open for 2% -> 3% of each run, Pallas kernels for 41% -> 16%
where the time goes in v2:
time: 246 us; the launch traced here: 245 us
  Pallas kernels  105 us (43%)
  blocking collectives  77.7 us (32%)
  waiting for transfers between devices  37.7 us (15%)
  starting transfers between devices  13.4 us (5%)
  local copies, waits for them, and re-layouts  5.06 us (2%)
  matrix products  4.85 us (2%)
    unnamed x1, blocking collectives  77.7 us
    pallas_call x1, Pallas kernels, factor(): pl.pallas_call(functools.partial(factor_kernel, part), out_shape=jax.Shap...  44.3 us
    pallas_call x1, Pallas kernels, local_part(): pl.pallas_call(local_kernel, out_shape=jax.ShapeDtypeStruct((arcs, 2, row...  40.1 us
    all_to_all x1, waiting for transfers between devices, per_device(): lax.all_to_all(packed, 'col', split_axis=0, concat_axis=0, tiled=True)  37.7 us
    pallas_call x1, Pallas kernels, eliminate(): pl.pallas_call(eliminate_kernel, out_shape=jax.ShapeDtypeStruct((groups,...  12.1 us
    pallas_call x1, Pallas kernels, layout(): pl.pallas_call(layout_kernel, out_shape=jax.ShapeDtypeStruct((arcs, packe...  8.06 us
    all_to_all x1, starting transfers between devices, per_device(): lax.all_to_all(kept, 'arc', split_axis=0, concat_axis=0, tiled=True)  7.61 us
    all_to_all x1, starting transfers between devices, per_device(): lax.all_to_all(packed, 'col', split_axis=0, concat_axis=0, tiled=True)  5.77 us
  transfers between devices with their start and end apart: 2, of which 1 were waited for; matrix products, arithmetic and copies ran while one was open for 3% of the time, Pallas kernels for 16%

profile of v2, /device:TPU:24, one launch (start us, length us, event | category | flops | bytes accessed | tf_op | source)
XLA Modules:
  0.0 244.6 jit_solution(11524390153597413962)
XLA Ops:
  0.0 0.0 copy-start
  0.0 8.1 %shard_map.55 = f32[128,80,128]{2,1,0:T(8,128)S(1)} custom-call(f32[320,32,128]{2,1,0:T(8,128)} %bitcast.5), custom_call_target="tpu_custom_call" | custom-call | tf_op jit(solution)/shard_map/pallas_call | solution.py:146
  8.1 0.0 copy-start.1
  8.1 2.3 copy-done.1
  10.4 5.8 %all-to-all-start = ((f32[128,80,128]{2,1,0:T(8,128)}), f32[128,80,128]{2,1,0:T(8,128)}, u32[]{:S(2)}, u32[]{:S(2)}) async-start(f32[128,80,128]{2,1,0:T(8,128)} %copy-done.1), calls=%async_computation | async-start | bytes 10485760 | tf_op jit(solution)/shard_map/all_to_all | solution.py:350
  16.1 0.0 copy-done.4
  16.2 0.1 dynamic_slice.3.counts_ref
  16.2 40.1 %shard_map.56.z_ref = bf16[8,2,320,512]{3,2,1,0:T(8,128)(2,1)} custom-call(s32[8]{0:T(128)S(1)} %dynamic_slice.3.counts_ref, f32[8,320,128]{2,1,0:T(8,128)S(1)} %copy-done.3), custom_call_target="tpu_custom_call" | custom-call | tf_op jit(solution)/shard_map/pallas_call | solution.py:206
  56.4 0.2 convert_reduce_fusion.1.slot_ref
  56.6 37.7 %all-to-all-done = f32[128,80,128]{2,1,0:T(8,128)} async-done(((f32[128,80,128]{2,1,0:T(8,128)}), f32[128,80,128]{2,1,0:T(8,128)}, u32[]{:S(2)}, u32[]{:S(2)}) %all-to-all-start) | async-done | bytes 5242912 | tf_op jit(solution)/shard_map/all_to_all | solution.py:350
  94.2 12.1 %shard_map.57 = f32[8,512,384]{2,1,0:T(8,128)} custom-call(s32[8]{0:T(128)S(1)} %and_select_fusion.dest_ref, s32[8]{0:T(128)S(1)} %convert_reduce_fusion.1.slot_ref, f32[16,8,80,128]{3,2,1,0:T(8,128)} %bitcast.2.g_ref, bf16[8,2,320,512]{3,2,1,0:T(8,128)(2,1)} %shard_map.56.z_ref), custom_call_target="tpu_custom_call" | custom-call | tf_op jit(solution)/shard_map/pallas_call | solution.py:250
  106.3 7.6 %all-to-all-start.1 = ((f32[8,512,384]{2,1,0:T(8,128)}), f32[8,512,384]{2,1,0:T(8,128)}, u32[]{:S(2)}, u32[]{:S(2)}) async-start(f32[8,512,384]{2,1,0:T(8,128)} %shard_map.57), calls=%async_computation.1 | async-start | bytes 12582912 | tf_op jit(solution)/shard_map/all_to_all | solution.py:362
  113.9 0.6 dynamic-slice
  115.2 0.2 dynamic-update-slice
  115.4 77.7 %all-reduce = s32[64]{0:T(128)S(1)} all-reduce(s32[64]{0:T(128)S(1)} %dynamic-update-slice), channel_id=2, replica_groups=mesh['arc'=8,'col'=16] {'arc'}, use_global_device_ids=true, to_apply=%add | all-reduce | flops 64 | bytes 512
  193.1 0.1 reshape.28
  193.2 0.3 convert_reduce_fusion
  193.5 0.1 select_reduce_fusion
  193.6 0.1 copy.8
  193.7 0.1 sub.25.labels_ref
  193.8 4.9 %fusion.6.refs_1_ = f32[2,512,512]{2,1,0:T(8,128)} fusion(f32[2,512,512]{2,1,0:T(8,128)S(1)} %copy-done), kind=kOutput, calls=%fused_computation.32 | convolution fusion | flops 3221225472 | bytes 4194304 | tf_op jit(solution)/shard_map/sij,sik->sjk/dot_general | solution.py:358
  198.7 0.0 all-to-all-done.1.refs_0_
  198.7 1.6 copy-done.2
  200.3 44.3 %shard_map.58 = f32[2,512,512]{2,1,0:T(8,128)} custom-call(s32[16]{0:T(128)S(1)} %sub.25.labels_ref, f32[8,512,384]{2,1,0:T(8,128)} %all-to-all-done.1.refs_0_, f32[2,512,512]{2,1,0:T(8,128)S(1)} %copy-done.2), custom_call_target="tpu_custom_call" | custom-call | tf_op jit(solution)/shard_map/pallas_call | solution.py:318
  (15 shorter events, 0.1 us)
Async XLA Ops:
  0.0 193.8 %copy-start = (f32[2,512,512]{2,1,0:T(8,128)S(1)}, f32[2,512,512]{2,1,0:T(8,128)}, u32[]{:S(2)}) copy-start(f32[2,512,512]{2,1,0:T(8,128)} %param.9) | copy-start | bytes 6291460
  8.1 2.3 copy-start.1
  10.4 5.8 %copy-start.4 = (s32[128]{0:T(128)S(1)}, s32[128]{0:T(128)}, u32[]{:S(2)}) copy-start(s32[128]{0:T(128)} %param.7) | copy-start | bytes 1540
  10.4 5.9 %copy-start.3 = (f32[8,320,128]{2,1,0:T(8,128)S(1)}, f32[8,320,128]{2,1,0:T(8,128)}, u32[]{:S(2)}) copy-start(f32[8,320,128]{2,1,0:T(8,128)} %l_ref.1) | copy-start | bytes 3932164
  10.4 83.8 %all-to-all-start = ((f32[128,80,128]{2,1,0:T(8,128)}), f32[128,80,128]{2,1,0:T(8,128)}, u32[]{:S(2)}, u32[]{:S(2)}) async-start(f32[128,80,128]{2,1,0:T(8,128)} %copy-done.1), calls=%async_computation | async-start | bytes 10485760 | tf_op jit(solution)/shard_map/all_to_all | solution.py:350
  16.2 40.1 %copy-start.5 = (s32[8]{0:T(128)S(1)}, s32[8]{0:T(128)}, u32[]{:S(2)}) copy-start(s32[8]{0:T(128)} %param.8) | copy-start | bytes 100
  106.3 7.6 %copy-start.6 = (u32[128]{0:T(128)S(1)}, u32[128]{0:T(128)}, u32[]{:S(2)}) copy-start(u32[128]{0:T(128)} %constant.75) | copy-start | bytes 1540
  106.3 92.3 %all-to-all-start.1 = ((f32[8,512,384]{2,1,0:T(8,128)}), f32[8,512,384]{2,1,0:T(8,128)}, u32[]{:S(2)}, u32[]{:S(2)}) async-start(f32[8,512,384]{2,1,0:T(8,128)} %shard_map.57), calls=%async_computation.1 | async-start | bytes 12582912 | tf_op jit(solution)/shard_map/all_to_all | solution.py:362
  198.7 1.6 copy-start.2

commit v3 on v0

v3 whole, which is shorter than its diff:
```python
import functools

import jax
import jax.numpy as jnp
from jax import lax
from jax.experimental import pallas as pl
from jax.experimental.pallas import tpu as pltpu
from jax.sharding import PartitionSpec as P

SLICE_DEV = 2
HI = lax.Precision.HIGHEST
F32 = jnp.float32
BF16 = jnp.bfloat16
NN = (((1,), (0,)), ((), ()))
NT = (((1,), (1,)), ((), ()))
TN = (((0,), (0,)), ((), ()))
VMEM_LIMIT = 48 * 1024 * 1024


def dot(a, b, dims, precision=None):
    return lax.dot_general(a, b, dims, precision=precision, preferred_element_type=F32)


def split2(x):
    high = x.astype(BF16)
    return high, (x - high.astype(F32)).astype(BF16)


def dot3(a, b, dims):
    ah, al = a
    bh, bl = b
    return dot(ah, bh, dims) + (dot(ah, bl, dims) + dot(al, bh, dims))


def split3(x):
    high = x.astype(BF16).astype(F32)
    rest = x - high
    mid = rest.astype(BF16).astype(F32)
    return high, mid, rest - mid


def outer6(left, right):
    lh, lm, ll = split3(left)
    rh, rm, rl = split3(right)
    a = jnp.concatenate([lh, lh, lm, lh, ll, lm], axis=0).astype(BF16)
    b = jnp.concatenate([rh, rm, rh, rl, rh, rm], axis=0).astype(BF16)
    return dot(a, b, TN)


def outer3(left, right):
    lh, lm, _ = split3(left)
    rh, rm, _ = split3(right)
    a = jnp.concatenate([lh, lh, left - lh], axis=0).astype(BF16)
    b = jnp.concatenate([rh, right - rh, rh], axis=0).astype(BF16)
    return dot(a, b, TN)


def row_of(x, i):
    return jnp.broadcast_to(x[:, i : i + 1, :], x.shape)


def lane_of(x, i):
    return jnp.broadcast_to(x[:, :, i : i + 1], x.shape)


def panel_rows(p):
    return pl.ds(pl.multiple_of(8 * p, 8), 8)


def places(x, p):
    lane = lax.broadcasted_iota(jnp.int32, x.shape, 2) - 8 * p
    return lane, lax.broadcasted_iota(jnp.int32, x.shape, 1)


def columns_of(x, p):
    turned = pltpu.roll(x, lax.rem(128 - 8 * p, 128), 2)
    return [lane_of(turned, l) for l in range(8)]


def batch_panel(x, following, p):
    lane, sub = places(x, p)
    inside = (lane >= 0) & (lane < 8)
    c = columns_of(x, p)
    n = columns_of(following, p)
    place = jnp.where(inside, (lane == sub).astype(F32), x)
    following = jnp.where(inside, 0.0, following)
    pivots = x
    for i in range(8):
        d = row_of(c[i], i)
        inv = pl.reciprocal(d, approx=True)
        pivots = jnp.where(sub == i, d, pivots)
        below = jnp.where(sub > i, c[i], 0.0)
        below_n = n[i]
        for l in range(i + 1, 8):
            r = row_of(c[l], i)
            c[l] = c[l] - (below * r) * inv
            n[l] = n[l] - (below_n * r) * inv
        below = below * inv
        r = row_of(place, i)
        place = place - below * r
        following = following - (below_n * inv) * r
    scale = lax.rsqrt(pivots)
    return place * scale, following


def cholesky_batch(a_ref):
    count = a_ref.shape[0]

    def step(p, carry):
        left, right, x = carry
        a = a_ref[...]
        at_lane, at_row = places(a, p)
        t = jnp.stack([outer6(left[b], right[b]) for b in range(count)], axis=0)
        cleared = (at_lane < 0) & (at_lane >= -8) & (at_row >= 8 * p + 8)
        a_ref[...] = jnp.where(cleared, 0.0, a) - t
        following = a_ref[:, panel_rows(jnp.minimum(p + 1, 15)), :]
        place, following = batch_panel(x, following, p)
        lane, sub = places(x, p)
        a_ref[:, panel_rows(p), :] = place
        return jnp.where(lane >= 16, place, 0.0), place, following

    first = a_ref[:, :8, :]
    lax.fori_loop(0, 16, step, (jnp.zeros_like(first), jnp.zeros_like(first), first))


def columns_at(x, p):
    return [lane_of(x, 8 * p + l) for l in range(8)]


def cholesky_panel(x, c, following, p):
    lane, sub = places(x, p)
    inside = (lane >= 0) & (lane < 8)
    c = list(c)
    place = jnp.where(inside, (lane == sub).astype(F32), x)
    n = ahead = None
    if following is not None:
        n = columns_at(following, p)
        ahead = columns_at(following, p + 1)
        following = jnp.where(inside, 0.0, following)
    upper = x
    pivots = x
    for i in range(8):
        d = row_of(c[i], i)
        inv = pl.reciprocal(d, approx=True)
        pivots = jnp.where(sub == i, d, pivots)
        below = jnp.where(sub > i, c[i], 0.0)
        for l in range(i + 1, 8):
            r = row_of(c[l], i) * inv
            c[l] = c[l] - below * r
            if n is not None:
                n[l] = n[l] - n[i] * r
        r = row_of(place, i) * inv
        place = place - below * r
        if n is not None:
            following = following - n[i] * r
            less = n[i] * inv
            ahead = [ahead[l] - less * row_of(n[i], l) for l in range(8)]
        upper = upper - below * (row_of(upper, i) * inv)
    scale = lax.rsqrt(pivots)
    return upper * scale, place * scale, following, ahead


def cholesky_blocks(a_ref, store_upper):
    count = a_ref.shape[0]
    rows = [a_ref[:, 8 * q : 8 * q + 8, :] for q in range(16)]
    c = columns_at(rows[0], 0)
    for p in range(16):
        following = rows[p + 1] if p < 15 else None
        upper, place, following, c = cholesky_panel(rows[p], c, following, p)
        lane, sub = places(place, p)
        inside = (lane >= 0) & (lane < 8)
        a_ref[:, 8 * p : 8 * p + 8, :] = place
        if store_upper is not None:
            store_upper(p, jnp.where(lane >= sub, upper, 0.0))
        if p < 15:
            rows[p + 1] = following
        if p < 14:
            left = jnp.where(lane >= 16, place, 0.0)
            t = [outer3(left[b], place[b]) for b in range(count)]
            for q in range(p + 2, 16):
                part = jnp.stack([v[8 * q : 8 * q + 8] for v in t], axis=0)
                rows[q] = jnp.where(inside, 0.0, rows[q]) - part


def inverse_panel(a_ref, sign_ref, p):
    x = a_ref[:, panel_rows(p), :]
    lane, sub = places(x, p)
    c = columns_of(x, p)
    place = jnp.where((lane >= 0) & (lane < 8), (lane == sub).astype(F32), x)
    signs = sign_ref[...]
    for i in range(8):
        pv = row_of(c[i], i)
        s = jnp.where(pv >= 0.0, -1.0, 1.0)
        signs = jnp.where(lane == i, s, signs)
        inv = pl.reciprocal(pv - s, approx=True)
        lm = jnp.where(sub == i, 1.0 - inv, c[i] * inv)
        for l in range(i + 1, 8):
            c[l] = c[l] - lm * row_of(c[l], i)
        place = place - lm * row_of(place, i)
    sign_ref[...] = signs
    a = a_ref[...]
    at_lane, at_row = places(a, p)
    wide = jnp.concatenate([place] * 16, axis=1)
    factor = jnp.where((at_row >= 8 * p) & (at_row < 8 * p + 8), wide, 0.0)
    t = jnp.stack([dot(a[b], factor[b], NN, HI) for b in range(x.shape[0])], axis=0)
    a_ref[...] = jnp.where((at_lane >= 0) & (at_lane < 8), 0.0, a) - t
    a_ref[:, panel_rows(p), :] = place


def layout_kernel(x_ref, o_ref):
    rows, cols, arcs = x_ref.shape
    half = cols // 2
    for j in range(half):
        first = x_ref[:, j, :]
        second = x_ref[:, j + half, :]
        for tile in range(2):
            o_ref[:, tile * cols + j, :] = first[tile * 128 : tile * 128 + 128].T
            o_ref[:, tile * cols + j + half, :] = second[tile * 128 : tile * 128 + 128].T
        o_ref[:, 2 * cols + j, :] = jnp.concatenate([first[256:], second[256:]], axis=0).T


def layout(x):
    rows, cols, arcs = x.shape
    packed = 2 * cols + cols // 2
    return pl.pallas_call(
        layout_kernel,
        out_shape=jax.ShapeDtypeStruct((arcs, packed, 128), F32),
        compiler_params=pltpu.CompilerParams(vmem_limit_bytes=VMEM_LIMIT),
    )(x)


def local_kernel(counts_ref, l_ref, prior_ref, z_ref, info_ref, a_ref, q_ref, sign_ref):
    arcs, rows, loc = l_ref.shape
    place = lax.broadcasted_iota(jnp.int32, (rows, loc), 0)
    for b in range(arcs):
        masked = jnp.where(place < counts_ref[b], l_ref[b], 0.0)
        q_ref[b] = masked
        a_ref[b] = dot(masked, masked, TN, HI)
    cholesky_batch(a_ref)
    r = lax.broadcasted_iota(jnp.int32, (loc, loc), 0)
    l = lax.broadcasted_iota(jnp.int32, (loc, loc), 1)
    for b in range(arcs):
        basis = dot(q_ref[b], jnp.where(l <= r, a_ref[b], 0.0), NT, HI)
        q_ref[b] = basis
        a_ref[b] = basis[:loc]
    sign_ref[...] = jnp.zeros_like(sign_ref)

    def invert(p, carry):
        inverse_panel(a_ref, sign_ref, p)
        return carry

    lax.fori_loop(0, loc // 8, invert, 0)
    rest = rows - loc
    unit = (place == lax.broadcasted_iota(jnp.int32, (rows, loc), 1)).astype(F32)
    r2 = lax.broadcasted_iota(jnp.int32, (rest, rows), 0)
    l2 = lax.broadcasted_iota(jnp.int32, (rest, rows), 1)
    for b in range(arcs):
        q = q_ref[b]
        n = dot(q[loc:], a_ref[b], NN, HI)
        v = q * sign_ref[b][0:1] - unit
        keep = (l2 == r2 + loc) & (l2 < counts_ref[b])
        z = dot(n, v, NT, HI) + keep.astype(F32)
        zh, zl = split2(jnp.concatenate([z, z[:, 256:]], axis=1))
        z_ref[b, 0] = zh
        z_ref[b, 1] = zl
    half = prior_ref.shape[1] // 2
    for s in range(prior_ref.shape[0]):
        top = prior_ref[s, :half, :]
        low = prior_ref[s, :, half:]
        info_ref[s, :half, :] = dot(top[:, :half], top, TN, HI)
        info_ref[s, half:, half:] = dot(low, low, TN, HI)
        info_ref[s, half:, :half] = jnp.zeros((half, half), F32)


def local_part(counts, local_obs, prior):
    arcs, rows, loc = local_obs.shape
    vmem = pl.BlockSpec(memory_space=pltpu.VMEM)
    return pl.pallas_call(
        local_kernel,
        out_shape=(
            jax.ShapeDtypeStruct((arcs, 2, rows - loc, 384), BF16),
            jax.ShapeDtypeStruct(prior.shape, F32),
        ),
        in_specs=[pl.BlockSpec(memory_space=pltpu.SMEM), vmem, vmem],
        out_specs=(vmem, vmem),
        scratch_shapes=[
            pltpu.VMEM((arcs, loc, loc), F32),
            pltpu.VMEM((arcs, rows, loc), F32),
            pltpu.VMEM((arcs, 8, loc), F32),
        ],
        compiler_params=pltpu.CompilerParams(vmem_limit_bytes=VMEM_LIMIT),
    )(counts, local_obs, prior)


def eliminate_kernel(dest_ref, slot_ref, label_ref, g_ref, z_ref, o_ref, main_ref, tail_ref, sems, tail_sem):
    sources, _, packed, _ = g_ref.shape
    part = packed * 2 // 5
    half = part // 2
    width = sources * part
    a = pl.program_id(0)

    @pl.when(a == 0)
    def _():
        tail_ref[...] = jnp.zeros_like(tail_ref)
        tail_ref[:, width:, :] = jnp.full((tail_ref.shape[0], 8, 128), -1.0, F32)

    slot = slot_ref[a]
    dest = dest_ref[a]
    z = [jnp.concatenate([z_ref[0, i], jnp.zeros((64, 384), BF16)], axis=0) for i in range(2)]
    g = [g_ref[:, 0, i * part : (i + 1) * part, :].reshape(width, 128) for i in range(2)]
    t = g_ref[:, 0, 2 * part :, :].reshape(width // 2, 128)
    first = lax.broadcasted_iota(jnp.int32, t.shape, 1) < 64
    body = dot3(split2(jnp.concatenate(g, axis=1)), [w[:, :256] for w in z], NT)
    ends = [dot3(split2(jnp.where(own, t, 0.0)), [w[:, 256:] for w in z], NT) for own in (first, ~first)]
    ends = jnp.stack([e.reshape(sources, half, 256) for e in ends], axis=1).reshape(width, 256)
    r = body + ends
    main_ref[a] = r[:, :128]
    pltpu.make_async_copy(
        main_ref.at[a], o_ref.at[dest, pl.ds(pl.multiple_of(width * slot, 8), width), :], sems.at[a]
    ).start()
    tail_ref[dest, :width, :] += pltpu.roll(r[:, 128:], 64 * slot, 1)
    labels = tail_ref[dest, width:, :]
    at = lax.broadcasted_iota(jnp.int32, labels.shape, 0)
    tail_ref[dest, width:, :] = jnp.where(at == slot, label_ref[a].astype(F32), labels)

    @pl.when(a == pl.num_programs(0) - 1)
    def _():
        ends_copy = pltpu.make_async_copy(tail_ref, o_ref.at[:, 2 * width :, :], tail_sem)
        ends_copy.start()
        for b in range(main_ref.shape[0]):
            pltpu.make_async_copy(main_ref.at[b], o_ref.at[0, :width, :], sems.at[b]).wait()
        ends_copy.wait()


def eliminate(dest, slot, label, g, z, groups):
    sources, arcs, packed, _ = g.shape
    width = sources * packed * 2 // 5
    smem = pl.BlockSpec(memory_space=pltpu.SMEM)
    return pl.pallas_call(
        eliminate_kernel,
        out_shape=jax.ShapeDtypeStruct((groups, 3 * width + 8, 128), F32),
        grid=(arcs,),
        in_specs=[
            smem,
            smem,
            smem,
            pl.BlockSpec((sources, 1, packed, 128), lambda a: (0, a, 0, 0)),
            pl.BlockSpec((1, *z.shape[1:]), lambda a: (a, 0, 0, 0)),
        ],
        out_specs=pl.BlockSpec(memory_space=pl.ANY),
        scratch_shapes=[
            pltpu.VMEM((arcs, width, 128), F32),
            pltpu.VMEM((groups, width + 8, 128), F32),
            pltpu.SemaphoreType.DMA((arcs,)),
            pltpu.SemaphoreType.DMA,
        ],
        compiler_params=pltpu.CompilerParams(vmem_limit_bytes=VMEM_LIMIT),
    )(dest, slot, label, g, z)


def factor_kernel(x_ref, prior_ref, out_ref, info_ref, a_ref):
    slices, width, _ = prior_ref.shape
    half = width // 2
    n = pl.program_id(0)

    @pl.when(n == 0)
    def _():
        info_ref[...] = prior_ref[...]

    labels = x_ref[0, 3 * width :, :]
    for slot in range(2):
        label = labels[slot, 0].astype(jnp.int32)

        @pl.when(label >= 0)
        def _():
            tail = x_ref[0, 2 * width : 3 * width, :]
            own = lax.broadcasted_iota(jnp.int32, tail.shape, 1) // 64 == slot
            main = x_ref[0, slot * width : (slot + 1) * width, :]
            h, l = split2(jnp.concatenate([main, jnp.where(own, tail, 0.0)], axis=1))
            info_ref[label, :half, :] += dot3((h[:half], l[:half]), (h, l), NT)
            info_ref[label, half:, half:] += dot3((h[half:], l[half:]), (h[half:], l[half:]), NT)

    @pl.when(n == pl.num_programs(0) - 1)
    def _():
        r = lax.broadcasted_iota(jnp.int32, (128, 128), 0)
        l = lax.broadcasted_iota(jnp.int32, (128, 128), 1)
        for k in range(width // 128):
            lo, hi = 128 * k, 128 * k + 128
            a_ref[...] = info_ref[:, lo:hi, lo:hi]
            if k:
                out_ref[:, lo:hi, :lo] = jnp.zeros((slices, 128, lo), F32)

            def store(p, rows):
                out_ref[:, lo + 8 * p : lo + 8 * p + 8, lo:hi] = rows

            cholesky_blocks(a_ref, store)
            for s in range(slices if hi < width else 0):
                inverse = split2(jnp.where(l <= r, a_ref[s], 0.0))
                u = dot3(inverse, split2(info_ref[s, lo:hi, hi:]), NN)
                out_ref[s, lo:hi, hi:] = u
                uh, ul = split2(u)
                for j in range(0, width - hi, 128):
                    left = (uh[:, j : j + 128], ul[:, j : j + 128])
                    info_ref[s, hi + j : hi + j + 128, hi + j :] -= dot3(left, (uh[:, j:], ul[:, j:]), TN)


def factor(arrived, prior_gram):
    slices, width, _ = prior_gram.shape
    whole = pl.BlockSpec(prior_gram.shape, lambda n: (0, 0, 0))
    return pl.pallas_call(
        factor_kernel,
        out_shape=jax.ShapeDtypeStruct(prior_gram.shape, F32),
        grid=(arrived.shape[0],),
        in_specs=[pl.BlockSpec((1, *arrived.shape[1:]), lambda n: (n, 0, 0)), whole],
        out_specs=whole,
        scratch_shapes=[
            pltpu.VMEM((slices, width, width), F32),
            pltpu.VMEM((slices, 128, 128), F32),
        ],
        compiler_params=pltpu.CompilerParams(vmem_limit_bytes=VMEM_LIMIT),
    )(arrived, prior_gram)


def per_device(local_obs, global_obs, row_counts, owner_map, prior_factor):
    arc_dev = local_obs.shape[0]
    arc_groups = lax.axis_size("arc")
    col_groups = lax.axis_size("col")
    counts = lax.dynamic_slice_in_dim(row_counts, lax.axis_index("col") * arc_dev, arc_dev)
    packed = layout(jnp.transpose(global_obs, (1, 2, 0)))
    columns = lax.all_to_all(packed, "col", split_axis=0, concat_axis=0, tiled=True)
    columns = columns.reshape(col_groups, arc_dev, *packed.shape[1:])
    order = jnp.arange(arc_dev, dtype=jnp.int32)
    dest = owner_map // SLICE_DEV // col_groups
    earlier = (dest[None, :] == dest[:, None]) & (order[None, :] < order[:, None])
    slot = jnp.sum(earlier.astype(jnp.int32), axis=1)
    z, prior_gram = local_part(counts, local_obs, prior_factor)
    kept = eliminate(dest, slot, owner_map % SLICE_DEV, columns, z, arc_groups)
    arrived = lax.all_to_all(kept, "arc", split_axis=0, concat_axis=0, tiled=True)
    return factor(arrived, prior_gram)


def solution(mesh):
    placed = (
        P(("arc", "col"), None, None),
        P("arc", None, "col"),
        P("arc"),
        P(("arc", "col")),
        P(("arc", "col"), None, None),
    )
    return jax.shard_map(
        per_device,
        mesh=mesh,
        in_specs=placed,
        out_specs=P(("arc", "col"), None, None),
        check_vma=False,
    )
```

time: 613 us -> 217 us (0.35)
  other arithmetic: 337 us -> 0.2 us
  blocking collectives: 0 us -> 82 us
  Pallas kernels: 0 us -> 80.8 us
  matrix products: 80.6 us -> 0 us
  waiting for transfers between devices: 115 us -> 39.1 us
  local copies, waits for them, and re-layouts: 49.6 us -> 5.64 us
  starting transfers between devices: 20.9 us -> 5.77 us
    another operation x21 -> x0, other arithmetic: 329 us -> none  [the longest x15 156 us: per_device(): factor_low = jnp.linalg.cholesky(information)]
    all_to_all x0 -> x1, blocking collectives: none -> 82 us  [per_device(): lax.all_to_all(kept, 'arc', split_axis=0, concat_axis=0, tiled=True)]
    pallas_call x0 -> x4, Pallas kernels: none -> 80.8 us  [the longest x1 37 us: local_part(): pl.pallas_call(local_kernel, out_shape=(jax.ShapeDtypeStruct((arcs, 2, ro...]
    all_to_all x3 -> x1, waiting for transfers between devices: 115 us -> 39.1 us  [per_device(): lax.all_to_all(packed, 'col', split_axis=0, concat_axis=0, tiled=True)]
    dot_general x6 -> x0, matrix products: 68.4 us -> none  [the longest x1 31.2 us: per_device(): jnp.einsum('nrw,nrv->nwv', arrived, arrived, precision=highest_precision)]
    all_to_all x3 -> x1, starting transfers between devices: 20.9 us -> 5.77 us  [per_device(): lax.all_to_all(packed, 'col', split_axis=0, concat_axis=0, tiled=True)]
    all_to_all x4 -> x0, local copies, waits for them, and re-layouts: 13.6 us -> none  [the longest x2 12.4 us: per_device(): lax.all_to_all(global_obs, 'col', split_axis=0, concat_axis=2, tiled=True)]
    another operation x7 -> x0, matrix products: 12.2 us -> none  [the longest x6 9.39 us: per_device(): factor_low = jnp.linalg.cholesky(information)]
  transfers between devices with their start and end apart: 3 -> 1, of which waited for: 1 -> 1; matrix products, arithmetic and copies ran while one was open for 37% -> 0% of each run, Pallas kernels for 0% -> 17%
where the time goes in v3:
time: 217 us; the launch traced here: 214 us
  blocking collectives  82 us (38%)
  Pallas kernels  80.8 us (37%)
  waiting for transfers between devices  39.1 us (18%)
  starting transfers between devices  5.77 us (3%)
  local copies, waits for them, and re-layouts  5.64 us (3%)
    all_to_all x1, blocking collectives, per_device(): lax.all_to_all(kept, 'arc', split_axis=0, concat_axis=0, tiled=True)  82 us
    all_to_all x1, waiting for transfers between devices, per_device(): lax.all_to_all(packed, 'col', split_axis=0, concat_axis=0, tiled=True)  39.1 us
    pallas_call x1, Pallas kernels, local_part(): pl.pallas_call(local_kernel, out_shape=(jax.ShapeDtypeStruct((arcs, 2, ro...  37 us
    pallas_call x1, Pallas kernels, factor(): pl.pallas_call(factor_kernel, out_shape=jax.ShapeDtypeStruct(prior_gram.s...  26.2 us
    pallas_call x1, Pallas kernels, eliminate(): pl.pallas_call(eliminate_kernel, out_shape=jax.ShapeDtypeStruct((groups,...  9.65 us
    pallas_call x1, Pallas kernels, layout(): pl.pallas_call(layout_kernel, out_shape=jax.ShapeDtypeStruct((arcs, packe...  7.91 us
    all_to_all x1, starting transfers between devices, per_device(): lax.all_to_all(packed, 'col', split_axis=0, concat_axis=0, tiled=True)  5.77 us
    unnamed x12, local copies, waits for them, and re-layouts  5.56 us
  transfers between devices with their start and end apart: 1, of which 1 were waited for; matrix products, arithmetic and copies ran while one was open for 0% of the time, Pallas kernels for 17%

profile of v3, /device:TPU:24, one launch (start us, length us, event | category | flops | bytes accessed | tf_op | source)
XLA Modules:
  0.0 213.6 jit_solution(6004360251693247027)
XLA Ops:
  0.0 7.9 %shard_map.55 = f32[128,80,128]{2,1,0:T(8,128)S(1)} custom-call(f32[320,32,128]{2,1,0:T(8,128)} %bitcast.2), custom_call_target="tpu_custom_call" | custom-call | tf_op jit(solution)/shard_map/pallas_call | solution.py:225
  7.9 0.0 copy-start
  7.9 2.3 %copy-done = f32[128,80,128]{2,1,0:T(8,128)} copy-done((f32[128,80,128]{2,1,0:T(8,128)}, f32[128,80,128]{2,1,0:T(8,128)S(1)}, u32[]{:S(2)}) %copy-start) | copy-done | bytes 5242904
  10.2 0.0 copy-start.4
  10.2 0.0 copy-start.3
  10.2 0.0 copy-start.5
  10.2 5.8 %all-to-all-start = ((f32[128,80,128]{2,1,0:T(8,128)}), f32[128,80,128]{2,1,0:T(8,128)}, u32[]{:S(2)}, u32[]{:S(2)}) async-start(f32[128,80,128]{2,1,0:T(8,128)} %copy-done), calls=%async_computation | async-start | bytes 10485760 | tf_op jit(solution)/shard_map/all_to_all | solution.py:430
  16.0 0.0 copy-done.4
  16.0 0.1 dynamic_slice.3.counts_ref
  16.1 0.0 copy-done.3
  16.1 0.0 copy-start.2
  16.1 1.6 copy-done.2
  17.7 37.0 %shard_map.56 = (bf16[8,2,192,384]{3,2,1,0:T(8,128)(2,1)}, f32[2,512,512]{2,1,0:T(8,128)S(1)}) custom-call(s32[8]{0:T(128)S(1)} %dynamic_slice.3.counts_ref, f32[8,320,128]{2,1,0:T(8,128)S(1)} %copy-done.3, f32[2,512,512]{2,1,0:T(8,128)S(1)} %copy-done.2), custom_call_target="tpu_custom_call" | custom-call | tf_op jit(solution)/shard_map/pallas_call | solution.py:278
  54.7 0.0 copy-done.5
  54.8 0.2 convert_reduce_fusion.slot_ref
  54.9 39.1 %all-to-all-done = f32[128,80,128]{2,1,0:T(8,128)} async-done(((f32[128,80,128]{2,1,0:T(8,128)}), f32[128,80,128]{2,1,0:T(8,128)}, u32[]{:S(2)}, u32[]{:S(2)}) %all-to-all-start) | async-done | bytes 5242912 | tf_op jit(solution)/shard_map/all_to_all | solution.py:430
  94.1 0.0 copy-start.1
  94.1 1.7 copy-done.1
  95.7 9.7 %shard_map.57 = f32[8,1544,128]{2,1,0:T(8,128)} custom-call(s32[8]{0:T(128)S(1)} %get-tuple-element.10.dest_ref, s32[8]{0:T(128)S(1)} %convert_reduce_fusion.slot_ref, s32[8]{0:T(128)S(1)} %get-tuple-element.9.label_ref, f32[16,8,80,128]{3,2,1,0:T(8,128)} %bitcast.1.g_ref, bf16[8,2,192,384]{3,2,1,0:T(8,128)(2,1)S(1)} %copy-done.1), custom_call_target="tpu_custom_call" | custom-call | tf_op jit(solution)/shard_map/pallas_call | solution.py:339
  105.4 82.0 %all_to_all.10.x_ref = f32[8,1544,128]{2,1,0:T(8,128)} all-to-all(f32[8,1544,128]{2,1,0:T(8,128)} %shard_map.57), channel_id=1, replica_groups=mesh['arc'=8,'col'=16] {'arc'}, dimensions={0} | all-to-all | bytes 12648448 | tf_op jit(solution)/shard_map/all_to_all | solution.py:438
  187.4 26.2 %shard_map.58 = f32[2,512,512]{2,1,0:T(8,128)} custom-call(f32[8,1544,128]{2,1,0:T(8,128)} %all_to_all.10.x_ref, f32[2,512,512]{2,1,0:T(8,128)S(1)} %get-tuple-element.8.prior_ref), custom_call_target="tpu_custom_call" | custom-call | tf_op jit(solution)/shard_map/pallas_call | solution.py:410
  (1 shorter events, 0.0 us)
Async XLA Ops:
  7.9 2.3 %copy-start = (f32[128,80,128]{2,1,0:T(8,128)}, f32[128,80,128]{2,1,0:T(8,128)S(1)}, u32[]{:S(2)}) copy-start(f32[128,80,128]{2,1,0:T(8,128)S(1)} %shard_map.55) | copy-start | bytes 15728644
  10.2 5.8 %copy-start.4 = (s32[128]{0:T(128)S(1)}, s32[128]{0:T(128)}, u32[]{:S(2)}) copy-start(s32[128]{0:T(128)} %param.7) | copy-start | bytes 1540
  10.2 5.9 %copy-start.3 = (f32[8,320,128]{2,1,0:T(8,128)S(1)}, f32[8,320,128]{2,1,0:T(8,128)}, u32[]{:S(2)}) copy-start(f32[8,320,128]{2,1,0:T(8,128)} %l_ref.1) | copy-start | bytes 3932164
  10.2 44.5 %copy-start.5 = (s32[8]{0:T(128)S(1)}, s32[8]{0:T(128)}, u32[]{:S(2)}) copy-start(s32[8]{0:T(128)} %param.8) | copy-start | bytes 100
  10.2 83.8 %all-to-all-start = ((f32[128,80,128]{2,1,0:T(8,128)}), f32[128,80,128]{2,1,0:T(8,128)}, u32[]{:S(2)}, u32[]{:S(2)}) async-start(f32[128,80,128]{2,1,0:T(8,128)} %copy-done), calls=%async_computation | async-start | bytes 10485760 | tf_op jit(solution)/shard_map/all_to_all | solution.py:430
  16.1 1.6 copy-start.2
  94.1 1.7 copy-start.1
